TPU v7x, 32 devices: a whole 2x2x4 slice. The times are simulated.
32 devices in a mesh: half: 2 (over core), row: 4 (over y, x), col: 4 (over z).
Axes of the slice: x: 2, y: 2, z: 4, core: 2. Of those that a mesh axis runs over, the one named last changes fastest.
Arguments:
- child_diag: float32 [2, 512, 512], P('half'), as said below
- child_panel: float32 [2, 32, 4, 128, 512], P('half', None, 'row'), may hold values from -18 to 18
- child_window: float32 [2, 32, 4, 128, 16, 4, 128], P('half', None, 'row', None, None, 'col'), may hold values from -6 to 6
- parent_diag: float32 [512, 512], replicated
- parent_lead_panel: float32 [48, 4, 2, 4, 16, 512], P(None, 'row', 'half', 'col'), may hold values from -24 to 24
- index_maps: int32 [2, 128], replicated, may hold values from 0 to 191, as said below
Outputs:
- parent_front: float32 [48, 4, 128, 8, 2, 4, 128], P(None, 'row', None, None, 'half', 'col')
- parent_factor: float32 [48, 4, 2, 4, 16, 512], P(None, 'row', 'half', 'col')
- parent_pivot: float32 [512, 512], replicated
Inputs may be any that keep to these rules, and one draw needn't show every extreme that they name: child_diag and parent_diag are symmetric and positive definite. For each child k and each group a, the entries index_maps[k, a * 8 + u] with 0 <= u < 8 equal q * 8 + ((u + s) mod 8) for a group target q and a turn s fixed within the group; groups a < 8 have q = a, later groups have distinct q that rise with a; over the 8 groups of a child the turns s, taken modulo 8, are all different; for each child some group a < 8 has a turn divisible by 8, and another group a < 8 has a turn that leaves 1 modulo 8.
All inputs are finite; a program needn't handle non-finite values.
Results may differ from a plain program's by a relative error of at most 0.0001.
Values sent between devices are 32-bit elements; how exact they have to be, the bound alone decides.
A program may use at most 256 MiB of HBM per device.

v0:
```python
import jax
import jax.numpy as jnp
from jax import lax
from jax.sharding import PartitionSpec as P

BLOCK_EXTENT = 128
PB = 4
SB = 128
RB = 192
WB = 64


def from_root(shard, axis, root):
    mine = lax.axis_index(axis) == root
    return lax.psum(jnp.where(mine, shard, jnp.zeros_like(shard)), axis)


def pick_ranked(owners, values, wanted, slot_count, missing):
    matches = owners[..., None, :] == wanted[:, None]
    ranking = jnp.cumsum(matches.astype(jnp.int32), axis=-1) - 1
    slot_ids = jnp.arange(slot_count, dtype=jnp.int32)
    chosen = matches[..., None, :] & (ranking[..., None, :] == slot_ids[:, None])
    present = jnp.any(chosen, axis=-1)
    picked = jnp.sum(jnp.where(chosen, values[..., None, None, :], 0), axis=-1)
    return jnp.where(present, picked, missing)


def per_device(child_diag, child_panel, child_window, parent_diag, parent_lead_panel, index_maps):
    highest = lax.Precision.HIGHEST
    row_size = lax.axis_size("row")
    half_id = lax.axis_index("half")
    row_id = lax.axis_index("row")
    col_id = lax.axis_index("col")
    panel_width = PB * BLOCK_EXTENT
    group_size = 2 * row_size
    row_local = SB // row_size
    col_local = WB // row_size
    parent_row_blocks = RB // row_size
    parent_cols = WB // group_size
    per_row = 2 * (SB // group_size) // row_size
    per_col = (WB // group_size + row_size - 1) // row_size
    pivot_lower_factor = jnp.linalg.cholesky(parent_diag)
    own_rows = parent_lead_panel.reshape(-1, panel_width)
    solved = jax.scipy.linalg.solve_triangular(pivot_lower_factor, own_rows.T, lower=True).T
    parent_factor = solved.reshape(parent_lead_panel.shape)
    sub_rows = parent_lead_panel.shape[4]
    gathered = lax.all_gather(
        solved.reshape(parent_row_blocks, sub_rows, panel_width),
        ("half", "col"),
        axis=1,
        tiled=True,
    )
    paired = gathered[: 2 * parent_cols].reshape(parent_cols, 2, BLOCK_EXTENT, panel_width)
    offered = lax.dynamic_index_in_dim(paired, half_id, axis=1, keepdims=False)
    column_factor = from_root(offered, "row", col_id)
    child_low = jnp.linalg.cholesky(child_diag[0])
    child_rows = child_panel.reshape(-1, panel_width)
    child_factor = jax.scipy.linalg.solve_triangular(child_low, child_rows.T, lower=True).T
    leading = child_factor[: col_local * BLOCK_EXTENT]
    everyone = lax.all_gather(leading[None], "row", axis=0, tiled=True)
    child_columns = lax.dynamic_index_in_dim(everyone, col_id, axis=0, keepdims=False)
    schur_part = child_window.reshape(row_local * BLOCK_EXTENT, col_local * BLOCK_EXTENT) - jnp.dot(
        child_factor, child_columns.T, precision=highest
    )
    schur_blocks = schur_part.reshape(row_local, BLOCK_EXTENT, col_local, BLOCK_EXTENT)
    child_map = lax.dynamic_index_in_dim(index_maps, half_id, axis=0, keepdims=False)
    my_rows = lax.dynamic_index_in_dim(
        child_map.reshape(row_local, row_size), row_id, axis=1, keepdims=False
    )
    my_cols = lax.dynamic_index_in_dim(
        child_map[:WB].reshape(col_local, row_size), col_id, axis=1, keepdims=False
    )
    local_rows = jnp.arange(row_local, dtype=jnp.int32)
    local_cols = jnp.arange(col_local, dtype=jnp.int32)
    send_rows = pick_ranked(
        my_rows % row_size, local_rows, jnp.arange(row_size, dtype=jnp.int32), per_row, row_local
    )
    send_cols = pick_ranked(
        my_cols % group_size,
        local_cols,
        jnp.arange(group_size, dtype=jnp.int32),
        per_col,
        col_local,
    )
    all_rows = index_maps.reshape(2, row_local, row_size).transpose(0, 2, 1)
    row_target = pick_ranked(
        all_rows % row_size, all_rows // row_size, row_id[None], per_row, parent_row_blocks
    )[:, :, 0, :]
    all_cols = index_maps[:, :WB].reshape(2, col_local, row_size).transpose(0, 2, 1)
    col_target = pick_ranked(
        all_cols % group_size,
        all_cols // group_size,
        (half_id * row_size + col_id)[None],
        per_col,
        parent_cols,
    )[:, :, 0, :]
    assembled_front = jnp.zeros(
        (parent_row_blocks, BLOCK_EXTENT, parent_cols, BLOCK_EXTENT), jnp.float32
    )
    row_index = send_rows[None, :, None, :, None]
    col_index = send_cols.reshape(2, row_size, per_col)[:, None, :, None, :]
    outgoing = schur_blocks.at[row_index, :, col_index, :].get(mode="fill", fill_value=0.0)
    arrived = lax.all_to_all(
        outgoing.reshape(-1, per_row * per_col, BLOCK_EXTENT, BLOCK_EXTENT),
        ("half", "row", "col"),
        split_axis=0,
        concat_axis=0,
        tiled=True,
    )
    arrived = arrived.reshape(2, row_size, row_size, per_row, per_col, BLOCK_EXTENT, BLOCK_EXTENT)
    target_rows = row_target[:, :, None, :, None]
    target_cols = col_target[:, None, :, None, :]
    assembled_front = assembled_front.at[target_rows, :, target_cols, :].add(arrived, mode="drop")
    flat_front = assembled_front.reshape(
        parent_row_blocks * BLOCK_EXTENT, parent_cols * BLOCK_EXTENT
    )
    updated = flat_front - jnp.dot(
        gathered.reshape(-1, panel_width),
        column_factor.reshape(-1, panel_width).T,
        precision=highest,
    )
    return (
        updated.reshape(parent_row_blocks, 1, BLOCK_EXTENT, parent_cols, 1, 1, BLOCK_EXTENT),
        parent_factor,
        pivot_lower_factor,
    )


def solution(mesh):
    in_specs = (
        P("half", None, None),
        P("half", None, "row", None, None),
        P("half", None, "row", None, None, "col", None),
        P(),
        P(None, "row", "half", "col", None, None),
        P(),
    )
    out_specs = (
        P(None, "row", None, None, "half", "col", None),
        P(None, "row", "half", "col", None, None),
        P(),
    )
    return jax.shard_map(
        per_device, mesh=mesh, in_specs=in_specs, out_specs=out_specs, check_vma=False
    )
```

profile of v0, /device:TPU:9, one launch (start us, length us, event | category | flops | bytes accessed | tf_op | source)
XLA Modules:
  0.0 1587.0 jit_solution(15410754357474827690)
XLA Ops:
  8.1 9.0 copy.114
  17.6 11.7 cholesky.286
  29.5 9.8 custom-call.37
  40.0 11.7 cholesky.305
  51.8 10.0 custom-call.38
  62.5 11.7 cholesky.326
  74.2 9.8 custom-call.39
  84.6 11.7 cholesky.343
  101.1 18.7 %while.2 = (s32[]{:T(128)}, f32[512,512]{1,0:T(8,128)S(1)}, s32[4,2]{0,1:T(2,128)S(1)}, f32[4,128,128]{2,1,0:T(8,128)S(1)}, s32[]{:T(128)}) while((s32[]{:T(128)}, f32[512,512]{1,0:T(8,128)S(1)}, s32[4,2]{0,1:T(2,128)S(1)}, f32[4,128,128]{2,1,0:T(8,128)S(1)}, s32[]{:T(128)}) %tuple.70), condition=%wide.while_cond, body=%wide.while_body.sunk | while | flops 2 | bytes 131189 | solution.py:58
  119.8 39.3 %custom-call.28 = f32[4,128,128]{1,2,0:T(8,128)S(1)} custom-call(f32[4,128,128]{2,1,0:T(8,128)S(1)} %get-tuple-element.11), custom_call_target="InvertDiagBlocksLowerTriangular" | custom-call | tf_op jit(solution)/shard_map/jit(_solve_triangular)/triangular_solve | solution.py:58
  159.1 3.5 fusion.17
  162.6 3.5 convolution_subtract_fusion.1
  166.2 1.9 fusion.57
  168.1 4.7 convolution_subtract_fusion
  172.9 1.9 fusion.55
  174.8 6.7 fusion.9
  184.9 2.5 slice.167
  192.4 153.8 %all-gather.6.cloned.1.call-done = f32[8192,512]{0,1:T(8,128)} async-done(((f32[2048,512]{0,1:T(8,128)}), f32[8192,512]{0,1:T(8,128)}) %all-gather.6.cloned.1.call-update) | async-done | bytes 16777232 | tf_op jit(solution)/shard_map/all_gather | solution.py:60
  346.2 20.4 %reshape.506 = f32[4,2048,512]{1,0,2:T(4,128)} reshape(f32[8192,512]{0,1:T(8,128)} %all-gather.6.cloned.1.call-done) | data formatting | bytes 33554432 | tf_op jit(solution)/shard_map/all_gather | solution.py:60
  366.6 9.0 constant_dynamic-slice_fusion.2
  375.6 69.1 %fusion = f32[512,8,16,128]{3,1,2,0:T(8,128)} fusion(f32[512,8,16,128]{3,2,1,0:T(8,128)} %bitcast.214, f32[128,4096]{1,0:T(8,128)S(1)} %copy-done.5, f32[128,4096]{1,0:T(8,128)S(1)} %copy-done.3, f32[128,4096]{1,0:T(8,128)S(1)} %copy-done.1, f32[128,4096]{1,0:T(8,128)S(1)} %fusion.17, f32[1,2048,512]{1,0,2:T(1,128)S(1)} %constant_dynamic-slice_fusion.2), kind=kOutput, calls=%fused_computation.7 | convolution fusion | flops 51554287616 | bytes 79691776 | tf_op jit(solution)/shard_map/dot_general | solution.py:62
  444.7 17.2 %copy.117 = f32[512,8,16,128]{3,2,1,0:T(8,128)S(1)} copy(f32[512,8,16,128]{3,1,2,0:T(8,128)} %fusion) | data formatting | bytes 67108864
  462.0 14.3 copy.105
  476.3 29.4 %gather_fusion = f32[512,128,128]{2,1,0:T(8,128)} fusion(f32[32,128,16,128]{3,1,2,0:T(8,128)} %copy.105, s32[512]{0:T(512)S(1)} %reshape.494), kind=kCustom, calls=%fused_computation | custom fusion | bytes 67112960 | tf_op jit(solution)/shard_map/gather | solution.py:102
  505.7 22.5 %broadcast_select_fusion = f32[32,16,128,128]{3,2,1,0:T(8,128)} fusion(f32[32,16,128,128]{3,2,1,0:T(8,128)} %bitcast.211, pred[32,16]{1,0:T(8,128)(4,1)S(1)} %copy.100), kind=kLoop, calls=%fused_computation.10 | loop fusion | flops 8388608 | bytes 67109376 | tf_op jit(solution)/shard_map/select_n | solution.py:102
  528.2 5.3 all-to-all-start
  533.8 1.9 copy.108
  539.5 11.7 cholesky.358
  551.3 9.8 custom-call.40
  563.7 11.7 cholesky.377
  575.4 10.2 custom-call.41
  587.2 11.7 cholesky.398
  599.0 9.8 custom-call.42
  610.2 11.9 cholesky.415
  628.2 11.7 while.3
  628.9 2.3 bitcast_dynamic-update-slice_fusion.5
  631.9 2.3 bitcast_dynamic-update-slice_fusion.5
  634.8 2.3 bitcast_dynamic-update-slice_fusion.5
  637.8 2.2 bitcast_dynamic-update-slice_fusion.5
  640.0 39.3 %custom-call.29 = f32[4,128,128]{1,2,0:T(8,128)S(1)} custom-call(f32[4,128,128]{2,1,0:T(8,128)S(1)} %get-tuple-element.19), custom_call_target="InvertDiagBlocksLowerTriangular" | custom-call | tf_op jit(solution)/shard_map/jit(_solve_triangular)/triangular_solve | solution.py:44
  687.8 256.9 %all-gather.4.cloned.1.call-done = f32[48,128,512]{2,1,0:T(8,128)} async-done(((f32[48,16,512]{2,1,0:T(8,128)}), f32[48,128,512]{2,1,0:T(8,128)}) %all-gather.4.cloned.1.call-update) | async-done | bytes 12582928 | tf_op jit(solution)/shard_map/all_gather | solution.py:47
  944.7 2.2 slice-done
  950.2 419.9 %all-to-all-done = f32[32,16,128,128]{3,2,1,0:T(8,128)} async-done(((f32[32,16,128,128]{3,2,1,0:T(8,128)}), f32[32,16,128,128]{3,2,1,0:T(8,128)}, u32[]{:S(2)}, u32[]{:S(2)}) %all-to-all-start) | async-done | bytes 33554464 | tf_op jit(solution)/shard_map/all_to_all | solution.py:103
  1370.1 12.1 broadcast_in_dim.123
  1382.2 106.5 %scatter_fusion = f32[48,128,8,128]{3,1,2,0:T(8,128)} fusion(f32[48,128,8,128]{3,1,2,0:T(8,128)} %broadcast_in_dim.123, s32[512]{0:T(512)S(1)} %reshape.500, f32[512,128,128]{2,1,0:T(8,128)} %bitcast.19), kind=kCustom, calls=%fused_computation.1 | custom fusion | flops 8388608 | bytes 100667392 | tf_op jit(solution)/shard_map/scatter-add | solution.py:113
  1488.8 25.7 %copy.106 = f32[48,128,8,128]{3,2,1,0:T(8,128)} copy(f32[48,128,8,128]{3,1,2,0:T(8,128)} %scatter_fusion) | data formatting | bytes 50331648 | tf_op jit(solution)/shard_map/scatter-add | solution.py:113
  1514.5 53.2 %fusion.1 = f32[768,8,8,128]{3,1,2,0:T(8,128)S(1)} fusion(f32[768,8,8,128]{3,2,1,0:T(8,128)} %bitcast.213, f32[6144,512]{1,0:T(8,128)} %bitcast.220, f32[1024,512]{1,0:T(8,128)} %all-reduce.3.cloned.1.call-done), kind=kOutput, calls=%fused_computation.9 | convolution fusion | flops 38660997120 | bytes 65011712 | tf_op jit(solution)/shard_map/dot_general | solution.py:117
  1567.7 11.5 copy.119
  (164 shorter events, 49.1 us)
Async XLA Ops:
  8.0 338.2 %all-gather.6.cloned.1.call-start = ((), (), s32[]{:S(2)}) async-start(), calls=%async_computation.3 | async-start | bytes 20971520 | tf_op jit(solution)/shard_map/all_gather | solution.py:60
  8.1 9.0 copy-start.6
  119.8 39.3 %copy-start.9 = (s32[4,2]{0,1:T(2,128)}, s32[4,2]{0,1:T(2,128)S(1)}, u32[]{:S(2)}) copy-start(s32[4,2]{0,1:T(2,128)S(1)} %get-tuple-element.209) | copy-start | bytes 100
  168.1 15.3 copy-start
  174.8 8.6 copy-start.2
  183.5 1.4 copy-start.4
  187.4 0.7 copy-start.11
  187.4 4.5 copy-start.12
  366.6 9.0 copy-start.1
  366.6 9.0 copy-start.3
  366.6 9.0 copy-start.5
  528.2 841.9 %all-to-all-start = ((f32[32,16,128,128]{3,2,1,0:T(8,128)}), f32[32,16,128,128]{3,2,1,0:T(8,128)}, u32[]{:S(2)}, u32[]{:S(2)}) async-start(f32[32,16,128,128]{3,2,1,0:T(8,128)} %broadcast_select_fusion), calls=%async_computation | async-start | bytes 67108864 | tf_op jit(solution)/shard_map/all_to_all | solution.py:103
  533.5 2.2 copy-start.7
  533.5 411.2 %all-gather.4.cloned.1.call-start = ((), (), s32[]{:S(2)}) async-start(), calls=%async_computation.1 | async-start | bytes 14155776 | tf_op jit(solution)/shard_map/all_gather | solution.py:47
  538.5 1.0 copy-start.8
  598.9 29.3 %copy-start.10 = (s32[4,2]{0,1:T(2,128)S(1)}, s32[4,2]{0,1:T(2,128)}, u32[]{:S(2)}) copy-start(s32[4,2]{0,1:T(2,128)} %copy-done.9) | copy-start | bytes 100
  687.8 826.7 %all-reduce.3.cloned.1.call-start = ((), (), s32[]{:S(2)}) async-start(), calls=%async_computation.2 | async-start | bytes 4194304 | tf_op jit(solution)/shard_map/psum | solution.py:15
  944.7 2.2 slice-start
Sparse Core Ops, SparseCore 0:
  187.6 158.5 all-gather.5
  948.7 241.0 all-reduce.2
Sparse Core Ops, SparseCore 1:
  687.9 256.8 all-gather.3
where the time goes:
time: 1600 us; the launch traced here: 1590 us
  waiting for transfers between devices  831 us (52%)
  other arithmetic  374 us (23%)
  local copies, waits for them, and re-layouts  184 us (12%)
  matrix products  161 us (10%)
  between operations  21.8 us (1%)
    all_to_all x1, waiting for transfers between devices, per_device(): lax.all_to_all(outgoing.reshape(-1, per_row * per_col, BLOCK_EXTENT, BLOC...  420 us
    all_gather x1, waiting for transfers between devices, per_device(): lax.all_gather(solved.reshape(parent_row_blocks, sub_rows, panel_width),...  257 us
    all_gather x1, waiting for transfers between devices, per_device(): everyone = lax.all_gather(leading[None], 'row', axis=0, tiled=True)  154 us
    scatter-add x1, other arithmetic, per_device(): assembled_front.at[target_rows, :, target_cols, :].add(arrived, mode='drop')  107 us
    another operation x14, other arithmetic, per_device(): pivot_lower_factor = jnp.linalg.cholesky(parent_diag)  78.8 us
    another operation x14, other arithmetic, per_device(): child_low = jnp.linalg.cholesky(child_diag[0])  78.7 us
    dot_general x1, matrix products, per_device(): jnp.dot(child_factor, child_columns.T, precision=highest)  69.1 us
    dot_general x1, matrix products, per_device(): jnp.dot(gathered.reshape(-1, panel_width), column_factor.reshape(-1, pane...  53.2 us
  transfers between devices with their start and end apart: 4, of which 3 were waited for; matrix products, arithmetic and copies ran while one was open for 19% of the time, Pallas kernels for 0%

commit v1 on v0

v1 whole, which is shorter than its diff:
```python
import jax
import jax.numpy as jnp
from jax import lax
from jax.experimental import pallas as pl
from jax.experimental.pallas import tpu as pltpu
from jax.sharding import PartitionSpec as P

EXTENT = 128
VMEM_BYTES = 48 * 1024 * 1024


def from_root(shard, axis, root):
    mine = lax.axis_index(axis) == root
    return lax.psum(jnp.where(mine, shard, jnp.zeros_like(shard)), axis)


def rank_among(first, second):
    size = first.shape[-1]
    before = jnp.arange(size)[None, :] < jnp.arange(size)[:, None]
    same = (first[..., :, None] == first[..., None, :]) & (second[..., :, None] == second[..., None, :])
    return jnp.sum((same & before).astype(jnp.int32), axis=-1)


def pack_kernel(row_to, row_slot, col_half, col_col, col_slot, w_ref, o_ref):
    count = col_half.shape[0]
    for j in range(count):
        o_ref[col_half[j], 0, col_col[j], 0, col_slot[j]] = w_ref[0, pl.ds(j, EXTENT, stride=count), :]


def pack(window, row_to, row_slot, col_half, col_col, col_slot, row_size, per_row, per_col):
    row_local, span, _ = window.shape
    block = (2, 1, row_size, 1, per_col, EXTENT, EXTENT)
    return pl.pallas_call(
        pack_kernel,
        out_shape=jax.ShapeDtypeStruct((2, row_size, row_size, per_row, per_col, EXTENT, EXTENT), jnp.float32),
        grid_spec=pltpu.PrefetchScalarGridSpec(
            num_scalar_prefetch=5,
            grid=(row_local,),
            in_specs=[pl.BlockSpec((1, span, EXTENT), lambda i, *_: (i, 0, 0))],
            out_specs=pl.BlockSpec(block, lambda i, to, slot, *_: (0, to[i], 0, slot[i], 0, 0, 0)),
        ),
        compiler_params=pltpu.CompilerParams(vmem_limit_bytes=VMEM_BYTES),
        cost_estimate=pl.CostEstimate(flops=0, bytes_accessed=8 * window.size, transcendentals=0),
        name="pack",
    )(row_to, row_slot, col_half, col_col, col_slot, window)


def split(value):
    high = value.astype(jnp.bfloat16)
    return high, (value - high.astype(jnp.float32)).astype(jnp.bfloat16)


def times_transpose(left, right):
    return lax.dot_general(left, right, (((1,), (1,)), ((), ())), preferred_element_type=jnp.float32)


def update_kernel(source, slot, present, f0_ref, f1_ref, p_ref, b_ref, o_ref, high, low):
    step = pl.program_id(0)

    @pl.when(step == 0)
    def _():
        for part in range(3):
            high[part], low[part] = split(b_ref[part])

    def product(value, part):
        a_high, a_low = split(value)
        return (
            times_transpose(a_low, high[part])
            + times_transpose(a_high, low[part])
            + times_transpose(a_high, high[part])
        )

    o_ref[0] = -product(p_ref[0], 2)
    for child, ref in enumerate((f0_ref, f1_ref)):

        @pl.when(present[child, step] > 0)
        def _(ref=ref, child=child):
            o_ref[0] -= product(ref[0, 0, 0], child)


def update(factors, parent, columns, source, slot, present):
    rows, _, width = parent.shape
    span = columns.shape[1]
    f_block = (1, 1, 1, EXTENT, width)
    return pl.pallas_call(
        update_kernel,
        out_shape=jax.ShapeDtypeStruct((rows, EXTENT, span), jnp.float32),
        grid_spec=pltpu.PrefetchScalarGridSpec(
            num_scalar_prefetch=3,
            grid=(rows,),
            in_specs=[
                pl.BlockSpec(f_block, lambda i, a, b, c: (0, a[0, i], b[0, i], 0, 0)),
                pl.BlockSpec(f_block, lambda i, a, b, c: (1, a[1, i], b[1, i], 0, 0)),
                pl.BlockSpec((1, EXTENT, width), lambda i, *_: (i, 0, 0)),
                pl.BlockSpec((3, span, width), lambda i, *_: (0, 0, 0)),
            ],
            out_specs=pl.BlockSpec((1, EXTENT, span), lambda i, *_: (i, 0, 0)),
            scratch_shapes=[pltpu.VMEM((3, span, width), jnp.bfloat16)] * 2,
        ),
        compiler_params=pltpu.CompilerParams(vmem_limit_bytes=VMEM_BYTES),
        cost_estimate=pl.CostEstimate(
            flops=18 * rows * EXTENT * span * width, bytes_accessed=16 * rows * EXTENT * width, transcendentals=0
        ),
        name="update",
    )(source, slot, present, factors, factors, parent, columns)


def add_kernel(source, slot, present, col_from, col_slot, w0_ref, w1_ref, u_ref, o_ref):
    step = pl.program_id(0)
    count = o_ref.shape[1] // EXTENT
    for q in range(count):
        value = u_ref[0, :, q * EXTENT : (q + 1) * EXTENT]
        for child, ref in enumerate((w0_ref, w1_ref)):
            block = ref[0, 0, col_from[child, q], 0, col_slot[child, q]]
            value += jnp.where(present[child, step] > 0, block, 0.0)
        o_ref[0, pl.ds(q, EXTENT, stride=count), :] = value


def add_blocks(arrived, updates, source, slot, present, col_from, col_slot):
    _, row_size, _, per_row, per_col, _, _ = arrived.shape
    rows, _, span = updates.shape
    w_block = (1, 1, row_size, 1, per_col, EXTENT, EXTENT)
    return pl.pallas_call(
        add_kernel,
        out_shape=jax.ShapeDtypeStruct((rows, span, EXTENT), jnp.float32),
        grid_spec=pltpu.PrefetchScalarGridSpec(
            num_scalar_prefetch=5,
            grid=(rows,),
            in_specs=[
                pl.BlockSpec(w_block, lambda i, a, b, *_: (0, a[0, i], 0, b[0, i], 0, 0, 0)),
                pl.BlockSpec(w_block, lambda i, a, b, *_: (1, a[1, i], 0, b[1, i], 0, 0, 0)),
                pl.BlockSpec((1, EXTENT, span), lambda i, *_: (i, 0, 0)),
            ],
            out_specs=pl.BlockSpec((1, span, EXTENT), lambda i, *_: (i, 0, 0)),
        ),
        compiler_params=pltpu.CompilerParams(vmem_limit_bytes=VMEM_BYTES),
        cost_estimate=pl.CostEstimate(
            flops=2 * updates.size, bytes_accessed=16 * updates.size, transcendentals=0
        ),
        name="add_blocks",
    )(source, slot, present, col_from, col_slot, arrived, arrived, updates)


def per_device(child_diag, child_panel, child_window, parent_diag, parent_lead_panel, index_maps):
    row_size = lax.axis_size("row")
    half_id = lax.axis_index("half")
    row_id = lax.axis_index("row")
    col_id = lax.axis_index("col")
    group = 2 * row_size
    row_local = child_window.shape[1]
    col_local = child_window.shape[4]
    width = child_panel.shape[-1]
    sub_rows = parent_lead_panel.shape[4]
    parent_rows = parent_lead_panel.shape[0]
    blocks = row_local * row_size
    lead = col_local * row_size
    parent_cols = lead // group
    per_row = 2 * (blocks // group) // row_size
    per_col = (lead // group + row_size - 1) // row_size

    lead_maps = index_maps[:, :lead]
    dealt = jnp.broadcast_to(jnp.arange(blocks, dtype=jnp.int32) % row_size, index_maps.shape)
    row_ranks = rank_among(index_maps % row_size, dealt)
    col_ranks = rank_among(lead_maps % group, dealt[:, :lead])

    def held(values, axis_id):
        mine = lax.dynamic_index_in_dim(values, half_id, axis=0, keepdims=False)
        return lax.dynamic_index_in_dim(mine.reshape(-1, row_size), axis_id, axis=1, keepdims=False)

    row_to = held(index_maps % row_size, row_id)
    row_slot = held(row_ranks, row_id)
    col_to = held(lead_maps % group, col_id)
    col_slot = held(col_ranks, col_id)
    outgoing = pack(
        child_window.reshape(row_local, EXTENT * col_local, EXTENT),
        row_to,
        row_slot,
        col_to // row_size,
        col_to % row_size,
        col_slot,
        row_size,
        per_row,
        per_col,
    )
    arrived = lax.all_to_all(
        outgoing.reshape(-1, per_row * per_col, EXTENT, EXTENT),
        ("half", "row", "col"),
        split_axis=0,
        concat_axis=0,
        tiled=True,
    ).reshape(outgoing.shape)

    gathered = lax.all_gather(
        parent_lead_panel.reshape(parent_rows, sub_rows, width), ("half", "col"), axis=1, tiled=True
    )
    paired = gathered[: 2 * parent_cols].reshape(parent_cols, 2, EXTENT, width)
    offered = lax.dynamic_index_in_dim(paired, half_id, axis=1, keepdims=False)
    column_panel = from_root(offered, "row", col_id)

    child_low = jnp.linalg.cholesky(child_diag[0])
    child_rows = child_panel.reshape(-1, width)
    child_factor = jax.scipy.linalg.solve_triangular(child_low, child_rows.T, lower=True).T
    child_blocks = child_factor.reshape(row_local, EXTENT, width)
    own = jnp.arange(row_local, dtype=jnp.int32)
    row_pick = (row_to == jnp.arange(row_size)[:, None, None]) & (row_slot == jnp.arange(per_row)[:, None])
    row_list = jnp.sum(jnp.where(row_pick, own, 0), axis=-1)
    wanted = jnp.arange(2)[:, None, None] * row_size + col_id
    col_pick = (held(lead_maps % group, row_id) == wanted) & (
        held(col_ranks, row_id) == jnp.arange(per_col)[:, None]
    )
    col_list = jnp.sum(jnp.where(col_pick, own[:col_local], 0), axis=-1)
    picked = jnp.concatenate(
        [
            jnp.broadcast_to(row_list[None], (2, row_size, per_row)),
            jnp.broadcast_to(col_list[:, None], (2, row_size, per_col)),
        ],
        axis=-1,
    )
    exchanged = lax.all_to_all(
        jnp.take(child_blocks, picked.reshape(group, -1), axis=0, mode="clip"),
        ("half", "row"),
        split_axis=0,
        concat_axis=0,
        tiled=True,
    ).reshape(2, row_size, per_row + per_col, EXTENT, width)

    pivot = jnp.linalg.cholesky(parent_diag)
    both = jnp.concatenate([gathered.reshape(-1, width), column_panel.reshape(-1, width)], axis=0)
    solved = jax.scipy.linalg.solve_triangular(pivot, both.T, lower=True).T
    parent = solved[: parent_rows * EXTENT].reshape(parent_rows, EXTENT, width)
    parent_columns = solved[parent_rows * EXTENT :]
    parent_factor = lax.dynamic_slice_in_dim(
        parent, (half_id * row_size + col_id) * sub_rows, sub_rows, axis=1
    )

    ids = jnp.arange(blocks, dtype=jnp.int32)
    row_match = index_maps[:, None, :] == (jnp.arange(parent_rows) * row_size + row_id)[:, None]
    present = jnp.any(row_match, axis=-1).astype(jnp.int32)
    row_from = jnp.sum(jnp.where(row_match, ids % row_size, 0), axis=-1)
    row_from_slot = jnp.sum(jnp.where(row_match, row_ranks[:, None, :], 0), axis=-1)
    targets = jnp.arange(parent_cols) * group + half_id * row_size + col_id
    col_match = lead_maps[:, None, :] == targets[:, None]
    col_from = jnp.sum(jnp.where(col_match, ids[:lead] % row_size, 0), axis=-1)
    col_from_slot = jnp.sum(jnp.where(col_match, col_ranks[:, None, :], 0), axis=-1)

    child_ids = jnp.arange(2)[:, None]
    child_columns = exchanged[child_ids, col_from, per_row + col_from_slot]
    columns = jnp.concatenate(
        [child_columns.reshape(2, -1, width), parent_columns[None]], axis=0
    )
    updates = update(exchanged, parent, columns, row_from, row_from_slot, present)
    front = add_blocks(arrived, updates, row_from, row_from_slot, present, col_from, col_from_slot)
    return (
        front.reshape(parent_rows, 1, EXTENT, parent_cols, 1, 1, EXTENT),
        parent_factor.reshape(parent_lead_panel.shape),
        pivot,
    )


def solution(mesh):
    in_specs = (
        P("half", None, None),
        P("half", None, "row", None, None),
        P("half", None, "row", None, None, "col", None),
        P(),
        P(None, "row", "half", "col", None, None),
        P(),
    )
    out_specs = (
        P(None, "row", None, None, "half", "col", None),
        P(None, "row", "half", "col", None, None),
        P(),
    )
    return jax.shard_map(
        per_device, mesh=mesh, in_specs=in_specs, out_specs=out_specs, check_vma=False
    )
```

time: 1600 us -> 1370 us (0.86)
  Pallas kernels: 0 us -> 224 us
  waiting for transfers between devices: 831 us -> 647 us
  other arithmetic: 374 us -> 261 us
  matrix products: 161 us -> 74.4 us
  local copies, waits for them, and re-layouts: 184 us -> 118 us
    psum x1, waiting for transfers between devices: 0.01 us -> 268 us  [from_root(): return lax.psum(jnp.where(mine, shard, jnp.zeros_like(shard)), axis)]
    all_to_all x1 -> x2, waiting for transfers between devices: 420 us -> 189 us  [the longest x1 189 us: per_device(): lax.all_to_all(jnp.take(child_blocks, picked.reshape(group, -1), axis=0,...]
    pallas_call x0 -> x3, Pallas kernels: none -> 224 us  [the longest x1 137 us: update(): pl.pallas_call(update_kernel, out_shape=jax.ShapeDtypeStruct((rows, EXTEN...]
    all_gather x2 -> x1, waiting for transfers between devices: 411 us -> 189 us  [per_device(): lax.all_gather(parent_lead_panel.reshape(parent_rows, sub_rows, width), (...]
    dot_general x2 -> x0, matrix products: 122 us -> none  [the longest x1 69.1 us: per_device(): jnp.dot(child_factor, child_columns.T, precision=highest)]
    scatter-add x1 -> x0, other arithmetic: 107 us -> none  [per_device(): assembled_front.at[target_rows, :, target_cols, :].add(arrived, mode='drop')]
    another operation x13, matrix products: 12.1 us -> 53 us  [the longest x7 47.5 us: per_device(): solved = jax.scipy.linalg.solve_triangular(pivot, both.T, lower=True).T]
    scatter-add x1 -> x0, local copies, waits for them, and re-layouts: 25.7 us -> none  [per_device(): assembled_front.at[target_rows, :, target_cols, :].add(arrived, mode='drop')]
  transfers between devices with their start and end apart: 4 -> 4, of which waited for: 3 -> 3; matrix products, arithmetic and copies ran while one was open for 19% -> 19% of each run, Pallas kernels for 0% -> 13%
where the time goes in v1:
time: 1370 us; the launch traced here: 1360 us
  waiting for transfers between devices  647 us (47%)
  other arithmetic  261 us (19%)
  Pallas kernels  224 us (16%)
  local copies, waits for them, and re-layouts  118 us (9%)
  matrix products  74.4 us (5%)
  between operations  20.2 us (1%)
    psum x1, waiting for transfers between devices, from_root(): return lax.psum(jnp.where(mine, shard, jnp.zeros_like(shard)), axis)  268 us
    all_to_all x1, waiting for transfers between devices, per_device(): lax.all_to_all(jnp.take(child_blocks, picked.reshape(group, -1), axis=0,...  189 us
    all_gather x1, waiting for transfers between devices, per_device(): lax.all_gather(parent_lead_panel.reshape(parent_rows, sub_rows, width), (...  189 us
    pallas_call x1, Pallas kernels, update(): pl.pallas_call(update_kernel, out_shape=jax.ShapeDtypeStruct((rows, EXTEN...  137 us
    another operation x14, other arithmetic, per_device(): child_low = jnp.linalg.cholesky(child_diag[0])  78.8 us
    another operation x14, other arithmetic, per_device(): pivot = jnp.linalg.cholesky(parent_diag)  78.7 us
    pallas_call x1, Pallas kernels, add_blocks(): pl.pallas_call(add_kernel, out_shape=jax.ShapeDtypeStruct((rows, span, EX...  47.8 us
    another operation x7, matrix products, per_device(): solved = jax.scipy.linalg.solve_triangular(pivot, both.T, lower=True).T  47.5 us
  transfers between devices with their start and end apart: 4, of which 3 were waited for; matrix products, arithmetic and copies ran while one was open for 19% of the time, Pallas kernels for 13%

profile of v1, /device:TPU:9, one launch (start us, length us, event | category | flops | bytes accessed | tf_op | source)
XLA Modules:
  0.0 1356.1 jit_solution(801749241816085474)
XLA Ops:
  13.9 11.7 cholesky.286
  25.6 9.8 custom-call.35
  36.2 11.7 cholesky.305
  48.0 10.0 custom-call.36
  58.6 11.7 cholesky.326
  71.1 9.8 custom-call.37
  81.5 11.9 cholesky.343
  97.4 8.5 while.2
  105.9 39.3 %custom-call.28 = f32[4,128,128]{1,2,0:T(8,128)S(1)} custom-call(f32[4,128,128]{2,1,0:T(8,128)S(1)} %get-tuple-element.11), custom_call_target="InvertDiagBlocksLowerTriangular" | custom-call | tf_op jit(solution)/shard_map/jit(_solve_triangular)/triangular_solve | solution.py:202
  145.2 8.9 copy.41
  157.7 3.6 convolution_subtract_fusion.3
  167.5 4.3 fusion.18
  173.8 3.9 maximum_bitcast_fusion.2
  177.7 9.0 copy.42
  186.7 13.8 %gather_fusion = f32[80,128,512]{2,1,0:T(8,128)} fusion(f32[32,128,512]{2,1,0:T(8,128)} %bitcast.143, s32[1024]{0:T(1024)S(1)} %pad_clamp_fusion), kind=kCustom, calls=%fused_computation | custom fusion | bytes 41943360 | tf_op jit(solution)/shard_map/jit(_take)/gather | solution.py:220
  200.5 6.6 all-to-all-start.1
  207.1 39.1 %pack.1 = f32[2,4,4,8,2,128,128]{6,5,4,3,2,1,0:T(8,128)} custom-call(s32[32]{0:T(128)S(1)} %dynamic-slice_reduce_fusion.1.row_to, s32[32]{0:T(128)S(1)} %dynamic-slice_reduce_fusion.row_slot, s32[16]{0:T(128)S(1)} %get-tuple-element.82.col_half, s32[16]{0:T(128)S(1)} %get-tuple-element.81.col_col, s32[16]{0:T(128)S(1)} %get-tuple-element.32.col_slot, ...), custom_call_target="tpu_custom_call" | custom-call | bytes 67108864 | tf_op jit(solution)/shard_map/pack/pallas_call | solution.py:33
  246.2 189.2 %all-to-all-done.1 = f32[8,10,128,512]{3,2,1,0:T(8,128)} async-done(((f32[8,10,128,512]{3,2,1,0:T(8,128)}), f32[8,10,128,512]{3,2,1,0:T(8,128)}, u32[]{:S(2)}, u32[]{:S(2)}) %all-to-all-start.1) | async-done | bytes 20971552 | tf_op jit(solution)/shard_map/all_to_all | solution.py:219
  435.3 4.6 all-to-all-start
  443.1 11.7 cholesky.358
  454.8 9.8 custom-call.38
  467.3 11.7 cholesky.377
  479.0 10.2 custom-call.39
  490.8 11.7 cholesky.398
  502.5 9.8 custom-call.40
  513.8 11.7 cholesky.415
  528.9 188.8 %all-gather.3.cloned.1.call-done = f32[48,1,1,1,128,512]{5,4,3,2,1,0:T(8,128)} async-done(((f32[48,1,1,1,16,512]{5,4,3,2,1,0:T(8,128)}), f32[48,1,1,1,128,512]{5,4,3,2,1,0:T(8,128)}) %all-gather.3.cloned.1.call-update) | async-done | bytes 12582928 | tf_op jit(solution)/shard_map/all_gather | solution.py:193
  726.4 7.7 while.3
  734.1 39.3 %custom-call.29 = f32[4,128,128]{1,2,0:T(8,128)S(1)} custom-call(f32[4,128,128]{2,1,0:T(8,128)S(1)} %get-tuple-element.19), custom_call_target="InvertDiagBlocksLowerTriangular" | custom-call | tf_op jit(solution)/shard_map/jit(_solve_triangular)/triangular_solve | solution.py:229
  773.6 9.8 gather_fusion.1
  783.4 12.6 copy.43
  796.0 268.0 %all-reduce.3.cloned.1.call-done = f32[1024,512]{0,1:T(8,128)} async-done(((f32[1024,512]{0,1:T(8,128)}), f32[1024,512]{0,1:T(8,128)}) %all-reduce.3.cloned.1.call-update) | async-done | bytes 2097168 | tf_op jit(solution)/shard_map/psum | solution.py:14
  1064.1 6.2 maximum_bitcast_fusion
  1070.3 5.5 copy-done
  1075.7 5.2 fusion.24
  1080.9 5.2 copy.34
  1086.1 6.7 convolution_subtract_fusion.1
  1092.8 5.2 fusion.50
  1098.0 5.6 copy.35
  1103.6 8.9 convolution_subtract_fusion
  1112.5 5.2 fusion.48
  1117.7 5.2 copy.36
  1122.9 10.4 fusion.6
  1133.3 6.1 fusion.47
  1139.4 5.7 maximum_bitcast_fusion.1
  1145.1 10.6 slice.182
  1163.9 137.5 %update.1.u_ref = f32[48,128,1024]{2,1,0:T(8,128)} custom-call(s32[2,48]{1,0:T(2,128)S(1)} %get-tuple-element.36.source, s32[2,48]{1,0:T(2,128)S(1)} %get-tuple-element.35.slot, s32[2,48]{1,0:T(2,128)S(1)} %convert_element_type.10.present, f32[2,4,10,128,512]{4,3,2,1,0:T(8,128)} %bitcast.21.f0_ref.f1_ref, f32[2,4,10,128,512]{4,3,2,1,0:T(8,128)} %bitcast.21.f0_ref.f1_ref, ...), custom_call_target="tpu_custom_call" | custom-call | flops 57982058496 | bytes 50331648 | tf_op jit(solution)/shard_map/update/pallas_call | solution.py:85
  1301.3 47.8 %add_blocks.1 = f32[48,1024,128]{2,1,0:T(8,128)} custom-call(s32[2,48]{1,0:T(2,128)S(1)} %get-tuple-element.36.source, s32[2,48]{1,0:T(2,128)S(1)} %get-tuple-element.35.slot, s32[2,48]{1,0:T(2,128)S(1)} %convert_element_type.10.present, s32[2,8]{1,0:T(2,128)S(1)} %get-tuple-element.34.col_from, s32[2,8]{1,0:T(2,128)S(1)} %get-tuple-element.33.col_slot, ...), custom_call_target="tpu_custom_call" | custom-call | flops 12582912 | bytes 100663296 | tf_op jit(solution)/shard_map/add_blocks/pallas_call | solution.py:123
  (145 shorter events, 64.8 us)
Async XLA Ops:
  157.6 5.6 copy-start.1
  200.5 234.9 %all-to-all-start.1 = ((f32[8,10,128,512]{3,2,1,0:T(8,128)}), f32[8,10,128,512]{3,2,1,0:T(8,128)}, u32[]{:S(2)}, u32[]{:S(2)}) async-start(f32[8,10,128,512]{3,2,1,0:T(8,128)} %bitcast.144), calls=%async_computation.1 | async-start | bytes 41943040 | tf_op jit(solution)/shard_map/all_to_all | solution.py:219
  435.3 5.6 copy-start.8
  435.3 6.2 copy-start.6
  435.3 866.0 %all-to-all-start = ((f32[32,16,128,128]{3,2,1,0:T(8,128)}), f32[32,16,128,128]{3,2,1,0:T(8,128)}, u32[]{:S(2)}, u32[]{:S(2)}) async-start(f32[32,16,128,128]{3,2,1,0:T(8,128)} %bitcast.142), calls=%async_computation | async-start | bytes 67108864 | tf_op jit(solution)/shard_map/all_to_all | solution.py:185
  440.0 277.7 %all-gather.3.cloned.1.call-start = ((), (), s32[]{:S(2)}) async-start(), calls=%async_computation.3 | async-start | bytes 14155776 | tf_op jit(solution)/shard_map/all_gather | solution.py:193
  440.7 623.4 %all-reduce.3.cloned.1.call-start = ((), (), s32[]{:S(2)}) async-start(), calls=%async_computation.2 | async-start | bytes 4194304 | tf_op jit(solution)/shard_map/psum | solution.py:14
  442.1 1.0 copy-start.7
  717.7 2.2 slice-start
  1070.2 5.5 copy-start
  1122.9 16.5 %copy-start.5 = (f32[128,7168]{0,1:T(8,128)S(1)}, f32[128,7168]{0,1:T(8,128)}, u32[]{:S(2)}) copy-start(f32[128,7168]{0,1:T(8,128)} %copy.36) | copy-start | bytes 11010052
  1133.3 6.1 copy-start.3
  1133.3 6.1 copy-start.4
  1155.7 4.7 copy-start.2
Sparse Core Ops, SparseCore 0:
  442.4 275.2 all-gather.2
  724.0 339.9 all-reduce.2
